TPU v7x, 32 devices: a whole 2x2x4 slice. The times are simulated.
32 devices in a mesh: grp: 4 (over z), sp: 8 (over y, x, core).
Axes of the slice: x: 2, y: 2, z: 4, core: 2. Of those that a mesh axis runs over, the one named last changes fastest.
Arguments:
- query_input: bfloat16 [4096, 4096], P(('grp', 'sp')), may hold values from -6 to 6
- key_input: bfloat16 [4096, 4096], P(('grp', 'sp')), may hold values from -6 to 6
- value_heads_input: bfloat16 [4096, 4096], P(('grp', 'sp')), may hold values from -6 to 6
- conv_weight: float32 [3, 4, 4096], P(None, None, 'sp'), may hold values from -3 to 3
- feature_map: bfloat16 [128, 1024], replicated, may hold values from -0.5 to 0.5
- out_gain: float32 [4096], P('sp'), may hold values from 0.25 to 1.75
Outputs:
- attended: bfloat16 [4096, 4096], P(('grp', 'sp'))
All inputs are finite; a program needn't handle non-finite values.
Results may differ from a plain program's by a relative error of at most 0.0052.
Values may be sent and summed in bfloat16 or wider, within the bound.
No kernel may reach another device: no remote copies, remote signals or barrier semaphores. Data moves between devices by JAX's collectives and lax.ppermute only.
A program may use at most 128 MiB of HBM per device.

v0:
```python
import jax
import jax.numpy as jnp
from jax import lax
from jax.sharding import PartitionSpec as P

H = 32
DH = 128
CONV = 4
BLOCK = 256


def passed_along(block, axis, distance):
    devices = range(lax.axis_size(axis))
    route = [(i - distance, i) for i in devices if i - distance in devices]
    return lax.ppermute(block, axis, route)


def entering(part, axis, combine, identity):
    place = lax.axis_index(axis)
    gathered = lax.all_gather(part, axis)
    state = jnp.zeros_like(part) + jnp.asarray(identity, part.dtype)

    def one(hop, state):
        return combine(state, lax.dynamic_index_in_dim(gathered, hop, 0, False))

    return lax.fori_loop(0, place, one, state)


def causal_conv(source, earlier, weights):
    tap_count = weights.shape[0]
    length = source.shape[0]
    padded = jnp.concatenate([earlier.astype(jnp.float32), source.astype(jnp.float32)], 0)
    summed = jnp.zeros(source.shape, jnp.float32)
    for tap_index in range(tap_count):
        row_begin = tap_count - 1 - tap_index
        summed = summed + weights[tap_index] * padded[row_begin : row_begin + length]
    return summed.astype(jnp.bfloat16)


def add_states(earlier_total, later_total):
    return earlier_total + later_total


def local(query_input, key_input, value_heads_input, conv_weight, feature_map, out_gain):
    head_count = H // lax.axis_size("sp")
    regrouped = (
        lax.all_to_all(query_input, "sp", split_axis=1, concat_axis=0, tiled=True),
        lax.all_to_all(key_input, "sp", split_axis=1, concat_axis=0, tiled=True),
        lax.all_to_all(value_heads_input, "sp", split_axis=1, concat_axis=0, tiled=True),
    )
    length = regrouped[0].shape[0]
    rim_rows = jnp.stack([member_rows[length - (CONV - 1) :] for member_rows in regrouped])
    earlier_rows = passed_along(rim_rows, "grp", 1)
    block_count = length // BLOCK
    blocked = tuple(
        (
            causal_conv(regrouped[member], earlier_rows[member], conv_weight[member]).reshape(
                block_count, BLOCK, head_count, DH
            )
            for member in range(3)
        )
    )
    causal_mask = lax.iota(jnp.int32, BLOCK)[None, :] <= lax.iota(jnp.int32, BLOCK)[:, None]

    def feature_pass(inputs):
        query_block, key_block, value_tile_rows = inputs
        query_featurized = jnp.maximum(
            jnp.einsum("bhd,dm->bhm", query_block, feature_map, preferred_element_type=jnp.float32),
            0.0,
        ).astype(jnp.bfloat16)
        key_featurized = jnp.maximum(
            jnp.einsum("bhd,dm->bhm", key_block, feature_map, preferred_element_type=jnp.float32),
            0.0,
        ).astype(jnp.bfloat16)
        scores = jnp.einsum(
            "bhm,chm->hbc", query_featurized, key_featurized, preferred_element_type=jnp.float32
        )
        scores = jnp.where(causal_mask[None], scores, 0.0).astype(jnp.bfloat16)
        local_part = jnp.einsum(
            "hbc,chd->bhd", scores, value_tile_rows, preferred_element_type=jnp.float32
        )
        state_increment = jnp.einsum(
            "fzp,fzu->zpu", key_featurized, value_tile_rows, preferred_element_type=jnp.float32
        )
        return (local_part, query_featurized, state_increment)

    local_parts, query_feats, updates = lax.map(feature_pass, blocked)
    group_total = jnp.sum(updates, 0)
    earlier_state = entering(group_total, "grp", add_states, jnp.zeros_like(group_total))
    gain_rows = out_gain.reshape(head_count, DH)

    def finish_block(running_state, inputs):
        query_featurized, state_increment, local_part = inputs
        carried_part = jnp.einsum(
            "srj,rje->sre",
            query_featurized.astype(jnp.float32),
            running_state,
            precision=lax.Precision.HIGHEST,
        )
        numerator = local_part + carried_part
        normed = (
            numerator
            * lax.rsqrt(jnp.mean(numerator * numerator, -1, keepdims=True) + 1e-06)
            * gain_rows
        )
        return (running_state + state_increment, normed.astype(jnp.bfloat16))

    _, finished = lax.scan(finish_block, earlier_state, (query_feats, updates, local_parts))
    attended_output = finished.reshape(length, head_count * DH)
    return lax.all_to_all(attended_output, "sp", split_axis=0, concat_axis=1, tiled=True)


def solution(mesh):
    placed = (
        P(("grp", "sp"), None),
        P(("grp", "sp"), None),
        P(("grp", "sp"), None),
        P(None, None, "sp"),
        P(),
        P("sp"),
    )
    return jax.shard_map(
        local, mesh=mesh, in_specs=placed, out_specs=P(("grp", "sp"), None), check_vma=False
    )
```

profile of v0, /device:TPU:0, one launch (start us, length us, event | category | flops | bytes accessed | tf_op | source)
XLA Modules:
  0.0 371.6 jit_solution(10916164779313120274)
XLA Ops:
  8.9 5.2 %all-to-all-start = ((bf16[128,8,512]{0,2,1:T(8,128)(2,1)}), bf16[128,8,512]{0,2,1:T(8,128)(2,1)S(1)}, u32[]{:S(2)}, u32[]{:S(2)}) async-start(bf16[128,8,512]{0,2,1:T(8,128)(2,1)} %bitcast.8), calls=%async_computation | async-start | bytes 2097152 | tf_op jit(solution)/shard_map/all_to_all | solution.py:49
  15.4 14.1 %all-to-all-done = bf16[128,8,512]{0,2,1:T(8,128)(2,1)S(1)} async-done(((bf16[128,8,512]{0,2,1:T(8,128)(2,1)}), bf16[128,8,512]{0,2,1:T(8,128)(2,1)S(1)}, u32[]{:S(2)}, u32[]{:S(2)}) %all-to-all-start) | async-done | bytes 1048608 | tf_op jit(solution)/shard_map/all_to_all | solution.py:49
  29.5 3.6 all-to-all-start.2
  34.4 14.0 %all-to-all-done.2 = bf16[128,8,512]{0,2,1:T(8,128)(2,1)S(1)} async-done(((bf16[128,8,512]{0,2,1:T(8,128)(2,1)}), bf16[128,8,512]{0,2,1:T(8,128)(2,1)S(1)}, u32[]{:S(2)}, u32[]{:S(2)}) %all-to-all-start.2) | async-done | bytes 1048608 | tf_op jit(solution)/shard_map/all_to_all | solution.py:48
  48.4 4.2 %all-to-all-start.1 = ((bf16[128,8,512]{0,2,1:T(8,128)(2,1)}), bf16[128,8,512]{0,2,1:T(8,128)(2,1)}, u32[]{:S(2)}, u32[]{:S(2)}) async-start(bf16[128,8,512]{0,2,1:T(8,128)(2,1)} %bitcast.12), calls=%async_computation.1 | async-start | bytes 2097152 | tf_op jit(solution)/shard_map/all_to_all | solution.py:47
  54.6 13.5 %all-to-all-done.1 = bf16[128,8,512]{0,2,1:T(8,128)(2,1)} async-done(((bf16[128,8,512]{0,2,1:T(8,128)(2,1)}), bf16[128,8,512]{0,2,1:T(8,128)(2,1)}, u32[]{:S(2)}, u32[]{:S(2)}) %all-to-all-start.1) | async-done | bytes 1048608 | tf_op jit(solution)/shard_map/all_to_all | solution.py:47
  73.0 3.5 collective-permute-start
  85.2 45.9 %while.39 = (s32[]{:T(128)}, f32[4,256,4,128]{1,3,2,0:T(8,128)}, bf16[4,256,4,1024]{3,1,2,0:T(8,128)(2,1)}, f32[4,4,1024,128]{3,2,1,0:T(8,128)}, bf16[4,256,4,12...) while((s32[]{:T(128)}, f32[4,256,4,128]{1,3,2,0:T(8,128)}, ...), condition=%wide.region_1.2_spmd.clone, body=%wide.region_0.1_spmd.clone.sunk | while | flops 1414070272 | bytes 19007076 | solution.py:87
  86.4 2.8 bitcast_dynamic-update-slice_fusion.4
  91.2 3.4 fusion.74
  98.1 2.6 bitcast_dynamic-update-slice_fusion.4
  102.7 3.3 fusion.74
  109.5 2.7 bitcast_dynamic-update-slice_fusion.4
  114.1 3.3 fusion.74
  120.9 2.7 bitcast_dynamic-update-slice_fusion.4
  125.6 3.3 fusion.74
  131.2 5.5 %reduce_sum.18 = f32[4,1024,128]{2,1,0:T(8,128)} reduce(f32[4,4,1024,128]{3,2,1,0:T(8,128)} %get-tuple-element.431, f32[]{:T(128)} %constant.58.clone.1), dimensions={0}, to_apply=%region_2.3 | reduce | flops 1572864 | bytes 10485764 | tf_op jit(solution)/shard_map/reduce_sum | solution.py:88
  136.7 149.6 %all-gather.3.cloned.1.call-done = f32[16,1024,128]{2,1,0:T(8,128)} async-done(((f32[4,1024,128]{2,1,0:T(8,128)}), f32[16,1024,128]{2,1,0:T(8,128)}) %all-gather.3.cloned.1.call-update) | async-done | bytes 8388624 | tf_op jit(solution)/shard_map/all_gather | solution.py:20
  289.8 52.7 %while.38 = (s32[]{:T(128)}, f32[4,1024,128]{1,2,0:T(8,128)S(1)}, bf16[4,256,4,128]{3,2,1,0:T(4,128)(2,1)}, f32[4,4,1024,128]{3,2,1,0:T(8,128)}, f32[4,256,4,128...) while((s32[]{:T(128)}, f32[4,1024,128]{1,2,0:T(8,128)S(1)}, ...), condition=%wide.region_7.8_spmd, body=%wide.region_5.7_spmd.sunk | while | flops 1611924480 | bytes 21778008 | solution.py:108
  289.9 3.9 %multiply_reduce_fusion.2 = (f32[256,4]{0,1:T(4,128)S(1)}, f32[256,4,128]{0,2,1:T(8,128)S(1)}) fusion(f32[4,1024,128]{1,2,0:T(8,128)S(1)} %get-tuple-element.437, bf16[4,256,4,1024]{3,1,2,0:T(8,128)(2,1)} %get-tuple-element.449, s32[]{:T(128)} %get-tuple-element.436, f32[4,256,4,128]{1,3,2,0:T(8,128)} %get-tuple-element.448), kind=kOutput, calls=%fused_computation.9.clone.1 | convolution fusion | flops 1611004928 | bytes 5248000 | tf_op jit(solution)/shard_map/while/body/eval_jaxpr/srj,rje->sre/dot_general | solution.py:94
  294.9 3.1 constant_dynamic-slice_fusion.7
  298.0 2.9 copy.70
  303.0 3.9 %multiply_reduce_fusion.2 = (f32[256,4]{0,1:T(4,128)S(1)}, f32[256,4,128]{0,2,1:T(8,128)S(1)}) fusion(f32[4,1024,128]{1,2,0:T(8,128)S(1)} %get-tuple-element.437, bf16[4,256,4,1024]{3,1,2,0:T(8,128)(2,1)} %get-tuple-element.449, s32[]{:T(128)} %get-tuple-element.436, f32[4,256,4,128]{1,3,2,0:T(8,128)} %get-tuple-element.448), kind=kOutput, calls=%fused_computation.9.clone.1 | convolution fusion | flops 1611004928 | bytes 5248000 | tf_op jit(solution)/shard_map/while/body/eval_jaxpr/srj,rje->sre/dot_general | solution.py:94
  308.1 3.1 constant_dynamic-slice_fusion.7
  311.2 2.9 copy.70
  316.2 3.9 %multiply_reduce_fusion.2 = (f32[256,4]{0,1:T(4,128)S(1)}, f32[256,4,128]{0,2,1:T(8,128)S(1)}) fusion(f32[4,1024,128]{1,2,0:T(8,128)S(1)} %get-tuple-element.437, bf16[4,256,4,1024]{3,1,2,0:T(8,128)(2,1)} %get-tuple-element.449, s32[]{:T(128)} %get-tuple-element.436, f32[4,256,4,128]{1,3,2,0:T(8,128)} %get-tuple-element.448), kind=kOutput, calls=%fused_computation.9.clone.1 | convolution fusion | flops 1611004928 | bytes 5248000 | tf_op jit(solution)/shard_map/while/body/eval_jaxpr/srj,rje->sre/dot_general | solution.py:94
  321.3 3.1 constant_dynamic-slice_fusion.7
  324.3 2.9 copy.70
  329.4 3.9 %multiply_reduce_fusion.2 = (f32[256,4]{0,1:T(4,128)S(1)}, f32[256,4,128]{0,2,1:T(8,128)S(1)}) fusion(f32[4,1024,128]{1,2,0:T(8,128)S(1)} %get-tuple-element.437, bf16[4,256,4,1024]{3,1,2,0:T(8,128)(2,1)} %get-tuple-element.449, s32[]{:T(128)} %get-tuple-element.436, f32[4,256,4,128]{1,3,2,0:T(8,128)} %get-tuple-element.448), kind=kOutput, calls=%fused_computation.9.clone.1 | convolution fusion | flops 1611004928 | bytes 5248000 | tf_op jit(solution)/shard_map/while/body/eval_jaxpr/srj,rje->sre/dot_general | solution.py:94
  334.4 3.1 constant_dynamic-slice_fusion.7
  337.5 2.9 copy.70
  344.0 18.8 %all_to_all.76 = bf16[8,128,512]{2,1,0:T(8,128)(2,1)S(1)} all-to-all(bf16[8,128,512]{2,1,0:T(8,128)(2,1)S(1)} %all_to_all.68), channel_id=1, replica_groups=mesh['grp'=4,'sp'=8] {'sp'}, dimensions={0} | all-to-all | bytes 2097152 | tf_op jit(solution)/shard_map/all_to_all | solution.py:110
  (93 shorter events, 62.3 us)
Async XLA Ops:
  6.5 7.5 %copy-start.4 = (bf16[128,4096]{1,0:T(8,128)(2,1)S(1)}, bf16[128,4096]{1,0:T(8,128)(2,1)}, u32[]{:S(2)}) copy-start(bf16[128,4096]{1,0:T(8,128)(2,1)} %param.13) | copy-start | bytes 3145732
  8.9 20.6 %all-to-all-start = ((bf16[128,8,512]{0,2,1:T(8,128)(2,1)}), bf16[128,8,512]{0,2,1:T(8,128)(2,1)S(1)}, u32[]{:S(2)}, u32[]{:S(2)}) async-start(bf16[128,8,512]{0,2,1:T(8,128)(2,1)} %bitcast.8), calls=%async_computation | async-start | bytes 2097152 | tf_op jit(solution)/shard_map/all_to_all | solution.py:49
  14.1 19.0 %copy-start.5 = (bf16[128,4096]{1,0:T(8,128)(2,1)S(1)}, bf16[128,4096]{1,0:T(8,128)(2,1)}, u32[]{:S(2)}) copy-start(bf16[128,4096]{1,0:T(8,128)(2,1)} %param.12) | copy-start | bytes 3145732
  29.5 18.9 %all-to-all-start.2 = ((bf16[128,8,512]{0,2,1:T(8,128)(2,1)}), bf16[128,8,512]{0,2,1:T(8,128)(2,1)S(1)}, u32[]{:S(2)}, u32[]{:S(2)}) async-start(bf16[128,8,512]{0,2,1:T(8,128)(2,1)} %bitcast.16), calls=%async_computation.2 | async-start | bytes 2097152 | tf_op jit(solution)/shard_map/all_to_all | solution.py:48
  33.0 19.7 %copy-start.7 = (f32[3,4,512]{2,1,0:T(4,128)S(1)}, f32[3,4,512]{2,1,0:T(4,128)}, u32[]{:S(2)}) copy-start(f32[3,4,512]{2,1,0:T(4,128)} %param.15) | copy-start | bytes 73732
  48.4 19.7 %all-to-all-start.1 = ((bf16[128,8,512]{0,2,1:T(8,128)(2,1)}), bf16[128,8,512]{0,2,1:T(8,128)(2,1)}, u32[]{:S(2)}, u32[]{:S(2)}) async-start(bf16[128,8,512]{0,2,1:T(8,128)(2,1)} %bitcast.12), calls=%async_computation.1 | async-start | bytes 2097152 | tf_op jit(solution)/shard_map/all_to_all | solution.py:47
  52.6 233.6 %all-gather.3.cloned.1.call-start = ((), (), s32[]{:S(2)}) async-start(), calls=%async_computation.4 | async-start | bytes 10485760 | tf_op jit(solution)/shard_map/all_gather | solution.py:20
  70.3 2.3 copy-start.3
  73.0 5.2 %collective-permute-start = (bf16[3,3,512]{2,1,0:T(4,128)(2,1)S(1)}, bf16[3,3,512]{2,1,0:T(4,128)(2,1)S(1)}, u32[]{:S(2)}, u32[]{:S(2)}) collective-permute-start(bf16[3,3,512]{2,1,0:T(4,128)(2,1)S(1)} %pad_maximum_fusion.3), channel_id=1, source_target_pairs={{0,8},{8,16},{16,24},{1,9},{9,17},{17,25},{2,10},{10,18},{18,26},{... | collective-permute-start | bytes 27656 | tf_op jit(solution)/shard_map/ppermute | solution.py:15
  81.2 2.0 copy-start.2
  83.1 2.1 copy-start.1
  286.6 1.3 copy-start
  287.9 1.9 copy-start.6
Sparse Core Ops, SparseCore 0:
  136.8 149.4 all-gather.2
where the time goes:
time: 375 us; the launch traced here: 372 us
  waiting for transfers between devices  191 us (51%)
  local copies, waits for them, and re-layouts  58.3 us (16%)
  matrix products  51.7 us (14%)
  other arithmetic  21.1 us (6%)
  blocking collectives  18.8 us (5%)
  starting transfers between devices  16.5 us (4%)
  between operations  13.6 us (4%)
    all_gather x1, waiting for transfers between devices, entering(): gathered = lax.all_gather(part, axis)  150 us
    dynamic_slice x8, local copies, waits for them, and re-layouts, local(): lax.scan(finish_block, earlier_state, (query_feats, updates, local_parts))  23.8 us
    all_to_all x1, blocking collectives, local(): lax.all_to_all(attended_output, 'sp', split_axis=0, concat_axis=1, tiled=...  18.8 us
    dot_general x4, matrix products, finish_block(): jnp.einsum('srj,rje->sre', query_featurized.astype(jnp.float32), running_...  15.7 us
    all_to_all x1, waiting for transfers between devices, local(): lax.all_to_all(value_heads_input, 'sp', split_axis=1, concat_axis=0, tile...  14.1 us
    all_to_all x1, waiting for transfers between devices, local(): lax.all_to_all(key_input, 'sp', split_axis=1, concat_axis=0, tiled=True)  14 us
    all_to_all x1, waiting for transfers between devices, local(): lax.all_to_all(query_input, 'sp', split_axis=1, concat_axis=0, tiled=True)  13.5 us
    dot_general x4, matrix products, feature_pass(): jnp.einsum('hbc,chd->bhd', scores, value_tile_rows, preferred_element_typ...  13.3 us
  transfers between devices with their start and end apart: 5, of which 4 were waited for; matrix products, arithmetic and copies ran while one was open for 2% of the time, Pallas kernels for 0%

commit v1 on v0

v1 whole, which is shorter than its diff:
```python
import functools

import jax
import jax.numpy as jnp
from jax import lax
from jax.experimental import pallas as pl
from jax.experimental.pallas import tpu as pltpu
from jax.sharding import Mesh
from jax.sharding import PartitionSpec as P

H = 32
DH = 128
BLOCK = 256
TAIL = 8
RIM = 16
GROUP = ("part", "sp")


def dot(a, b):
    return jnp.dot(a, b, preferred_element_type=jnp.float32)


def dot_nt(a, b):
    return lax.dot_general(a, b, (((1,), (1,)), ((), ())), preferred_element_type=jnp.float32)


def stage(rows_ref, halo, first, pad_ref):
    width = rows_ref.shape[-1]
    count = pad_ref.shape[0] - TAIL

    @pl.when(first)
    def _():
        pad_ref[:TAIL] = halo[RIM - TAIL :].astype(jnp.float32)

    @pl.when(jnp.logical_not(first))
    def _():
        pad_ref[:TAIL] = pad_ref[count:]

    pad_ref[TAIL:] = rows_ref[...].reshape(count, width).astype(jnp.float32)


def conv(pad_ref, weights, begin):
    total = jnp.zeros((BLOCK, pad_ref.shape[1]), jnp.float32)
    for tap in range(weights.shape[0]):
        row = TAIL + begin - tap
        total = total + weights[tap][None, :] * pad_ref[row : row + BLOCK]
    return total.astype(jnp.bfloat16)


def relu16(x):
    return jnp.maximum(x, 0.0).astype(jnp.bfloat16)


def totals_kernel(k_ref, v_ref, halo_ref, w_ref, map_t_ref, out_ref, k_pad, v_pad, state):
    step = pl.program_id(0)
    first = step == 0
    heads = state.shape[0]
    stage(k_ref, halo_ref[0], first, k_pad)
    stage(v_ref, halo_ref[1], first, v_pad)

    @pl.when(first)
    def _():
        state[...] = jnp.zeros_like(state)

    for begin in range(0, k_pad.shape[0] - TAIL, BLOCK):
        keys = conv(k_pad, w_ref[1], begin)
        values = conv(v_pad, w_ref[2], begin)
        for h in range(heads):
            cols = slice(h * DH, (h + 1) * DH)
            feats_t = relu16(dot_nt(map_t_ref[...], keys[:, cols]))
            state[h] += dot(feats_t, values[:, cols])

    @pl.when(step == pl.num_programs(0) - 1)
    def _():
        out_ref[...] = state[...].astype(jnp.bfloat16)


def span_kernel(
    q_ref, k_ref, v_ref, qk_halo, kv_halo, w_ref, map_ref, map_t_ref,
    part_ref, feat_ref, q_pad, k_pad, v_pad, state,
):
    first = pl.program_id(0) == 0
    heads = state.shape[0]
    stage(q_ref, qk_halo[0], first, q_pad)
    stage(k_ref, kv_halo[0], first, k_pad)
    stage(v_ref, kv_halo[1], first, v_pad)

    @pl.when(first)
    def _():
        state[...] = jnp.zeros_like(state)

    row = lax.broadcasted_iota(jnp.int32, (BLOCK, BLOCK), 0)
    col = lax.broadcasted_iota(jnp.int32, (BLOCK, BLOCK), 1)
    causal = col <= row
    for begin in range(0, k_pad.shape[0] - TAIL, BLOCK):
        rows = slice(begin, begin + BLOCK)
        queries = conv(q_pad, w_ref[0], begin)
        keys = conv(k_pad, w_ref[1], begin)
        values = conv(v_pad, w_ref[2], begin)
        for h in range(heads):
            cols = slice(h * DH, (h + 1) * DH)
            feats_t = relu16(dot_nt(map_t_ref[...], keys[:, cols]))
            feats = relu16(dot(queries[:, cols], map_ref[...]))
            feat_ref[h, rows] = feats
            scores = jnp.where(causal, dot(feats, feats_t), 0.0).astype(jnp.bfloat16)
            high = state[h].astype(jnp.bfloat16)
            low = (state[h] - high.astype(jnp.float32)).astype(jnp.bfloat16)
            carried = dot(feats, jnp.concatenate([high, low], 1))
            part_ref[rows, cols] = (
                dot(scores, values[:, cols]) + carried[:, :DH] + carried[:, DH:]
            )
            state[h] += dot(feats_t, values[:, cols])


def finish_kernel(part_ref, feat_ref, state_ref, gain_ref, out_ref):
    heads = state_ref.shape[0]
    for h in range(heads):
        cols = slice(h * DH, (h + 1) * DH)
        numerator = part_ref[:, cols] + dot(feat_ref[h], state_ref[h])
        scale = lax.rsqrt(jnp.mean(numerator * numerator, -1, keepdims=True) + 1e-06)
        out_ref[:, cols] = (numerator * scale * gain_ref[:, cols]).astype(jnp.bfloat16)


PARAMS = pltpu.CompilerParams(
    dimension_semantics=("arbitrary",), vmem_limit_bytes=40 * 1024 * 1024
)


def whole(array):
    zeros = (0,) * array.ndim
    return pl.BlockSpec(array.shape, lambda i: zeros)


def step_chunks(count, rows):
    per_block = BLOCK // rows
    return per_block * (2 if count % (2 * per_block) == 0 else 1)


def span_totals(kv, halo, weights, map_t):
    count, _, rows, width = kv.shape
    heads, chunks = width // DH, step_chunks(count, rows)
    features = map_t.shape[0]
    pad = pltpu.VMEM((TAIL + chunks * rows, width), jnp.float32)
    block = (chunks, 1, rows, width)
    shape = (heads, features, DH)
    return pl.pallas_call(
        totals_kernel,
        grid=(count // chunks,),
        in_specs=[
            pl.BlockSpec(block, lambda i: (i, 0, 0, 0)),
            pl.BlockSpec(block, lambda i: (i, 1, 0, 0)),
            whole(halo), whole(weights), whole(map_t),
        ],
        out_specs=pl.BlockSpec(shape, lambda i: (0, 0, 0)),
        out_shape=jax.ShapeDtypeStruct(shape, jnp.bfloat16),
        scratch_shapes=[pad, pad, pltpu.VMEM(shape, jnp.float32)],
        compiler_params=PARAMS,
        cost_estimate=pl.CostEstimate(
            flops=8 * count * rows * width * features, bytes_accessed=8 * count * rows * width,
            transcendentals=0,
        ),
    )(kv, kv, halo, weights, map_t)


def span_parts(queries, kv, q_halo, kv_halo, weights, feature_map, map_t):
    count, rows, width = queries.shape
    heads, chunks = width // DH, step_chunks(count, rows)
    features = map_t.shape[0]
    pad = pltpu.VMEM((TAIL + chunks * rows, width), jnp.float32)
    block = (chunks, 1, rows, width)
    tokens, step = count * rows, chunks * rows
    return pl.pallas_call(
        span_kernel,
        grid=(count // chunks,),
        in_specs=[
            pl.BlockSpec((chunks, rows, width), lambda i: (i, 0, 0)),
            pl.BlockSpec(block, lambda i: (i, 0, 0, 0)),
            pl.BlockSpec(block, lambda i: (i, 1, 0, 0)),
            whole(q_halo), whole(kv_halo), whole(weights), whole(feature_map), whole(map_t),
        ],
        out_specs=[
            pl.BlockSpec((step, width), lambda i: (i, 0)),
            pl.BlockSpec((heads, step, features), lambda i: (0, i, 0)),
        ],
        out_shape=[
            jax.ShapeDtypeStruct((tokens, width), jnp.float32),
            jax.ShapeDtypeStruct((heads, tokens, features), jnp.bfloat16),
        ],
        scratch_shapes=[pad, pad, pad, pltpu.VMEM((heads, features, DH), jnp.float32)],
        compiler_params=PARAMS,
        cost_estimate=pl.CostEstimate(
            flops=20 * tokens * width * features, bytes_accessed=24 * tokens * width,
            transcendentals=0,
        ),
    )(queries, kv, kv, q_halo, kv_halo, weights, feature_map, map_t)


def finished(parts, feats, state, gains):
    tokens, width = parts.shape
    heads, _, features = feats.shape
    step = tokens // 4
    return pl.pallas_call(
        finish_kernel,
        grid=(4,),
        in_specs=[
            pl.BlockSpec((step, width), lambda i: (i, 0)),
            pl.BlockSpec((heads, step, features), lambda i: (0, i, 0)),
            whole(state), whole(gains),
        ],
        out_specs=pl.BlockSpec((step, width), lambda i: (i, 0)),
        out_shape=jax.ShapeDtypeStruct((tokens, width), jnp.bfloat16),
        compiler_params=PARAMS,
        cost_estimate=pl.CostEstimate(
            flops=2 * tokens * width * features, bytes_accessed=24 * tokens * width,
            transcendentals=tokens,
        ),
    )(parts, feats, state, gains)


def next_span(block, spans):
    return lax.ppermute(block, "span", [(i, i + 1) for i in range(spans - 1)])


def local(spans, query_input, key_input, value_heads_input, conv_weight, feature_map, out_gain):
    rows, model = query_input.shape
    parts, members = lax.axis_size("part"), lax.axis_size("sp")
    count = parts * members
    width = model // count

    def by_owner(x):
        x = x.reshape(rows, members, parts, width)
        return x.transpose(2, 1, 0, 3).reshape(count, rows, width)

    kv = jnp.stack([by_owner(key_input), by_owner(value_heads_input)], 1)
    kv = lax.all_to_all(kv, GROUP, split_axis=0, concat_axis=0, tiled=True)
    queries = lax.all_to_all(by_owner(query_input), GROUP, split_axis=0, concat_axis=0, tiled=True)

    column = lax.axis_index("part") * width
    weights = lax.dynamic_slice_in_dim(conv_weight, column, width, 2)
    gains = lax.dynamic_slice_in_dim(out_gain, column, width, 0)[None]
    map_t = feature_map.T

    kv_rim = kv[count - 1, :, rows - RIM :]
    q_rim = queries[count - 1, None, rows - RIM :]
    rims = next_span(jnp.concatenate([kv_rim, q_rim], 0), spans)
    kv_halo, q_halo = rims[:2], rims[2:]

    if spans == 2:
        state = span_totals(kv, jnp.zeros_like(kv_halo), weights, map_t)
        earlier = next_span(state, spans)
    else:
        state = span_totals(kv, kv_halo, weights, map_t)
        gathered = lax.all_gather(state, "span")
        before = jnp.arange(spans) < lax.axis_index("span")
        earlier = jnp.sum(
            jnp.where(before[:, None, None, None], gathered.astype(jnp.float32), 0.0), 0
        ).astype(jnp.bfloat16)

    partial, feats = span_parts(queries, kv, q_halo, kv_halo, weights, feature_map, map_t)
    attended = finished(partial, feats, earlier, gains).reshape(count, rows, width)
    attended = lax.all_to_all(attended, GROUP, split_axis=0, concat_axis=0, tiled=True)
    attended = attended.reshape(parts, members, rows, width)
    return attended.transpose(2, 1, 0, 3).reshape(rows, model)


def solution(mesh):
    groups, members = mesh.devices.shape
    parts = 1
    while groups % (4 * parts) == 0 and H % (2 * parts * members) == 0:
        parts *= 2
    spans = groups // parts
    split = Mesh(mesh.devices.reshape(spans, parts, members), ("span", "part", "sp"))
    tokens = P(("span", "part", "sp"), None)
    placed = (tokens, tokens, tokens, P(None, None, "sp"), P(), P("sp"))
    return jax.shard_map(
        functools.partial(local, spans),
        mesh=split, in_specs=placed, out_specs=tokens, check_vma=False,
    )
```

time: 375 us -> 121 us (0.32)
  waiting for transfers between devices: 191 us -> 39.6 us
  matrix products: 51.7 us -> 0 us
  local copies, waits for them, and re-layouts: 58.3 us -> 11 us
  Pallas kernels: 0 us -> 25 us
  other arithmetic: 21.1 us -> 1.54 us
  between operations: 13.6 us -> 0.19 us
  blocking collectives: 18.8 us -> 27.5 us
    all_gather x1 -> x0, waiting for transfers between devices: 150 us -> none  [entering(): gathered = lax.all_gather(part, axis)]
    dot_general x20 -> x0, matrix products: 51.7 us -> none  [the longest x4 15.7 us: finish_block(): jnp.einsum('srj,rje->sre', query_featurized.astype(jnp.float32), running_...]
    dynamic_slice x20 -> x2, local copies, waits for them, and re-layouts: 33.5 us -> 0.08 us  [the longest x1 0.07 us: local(): gains = lax.dynamic_slice_in_dim(out_gain, column, width, 0)[None]]
    pallas_call x0 -> x3, Pallas kernels: none -> 25 us  [the longest x1 14.9 us: span_parts(): pl.pallas_call(span_kernel, grid=(count // chunks,), in_specs=[pl.BlockSp...]
    all_to_all x1, blocking collectives: 18.8 us -> 27.5 us  [local(): lax.all_to_all(attended, GROUP, split_axis=0, concat_axis=0, tiled=True)]
    add x4 -> x0, other arithmetic: 8.53 us -> none  [finish_block(): return (running_state + state_increment, normed.astype(jnp.bfloat16))]
    all_to_all x6 -> x0, local copies, waits for them, and re-layouts: 7.54 us -> none  [the longest x3 3.43 us: local(): lax.all_to_all(attended_output, 'sp', split_axis=0, concat_axis=1, tiled=...]
    convert_element_type x7 -> x0, other arithmetic: 6.42 us -> none  [the longest x3 3.62 us: causal_conv(): source.astype(jnp.float32)]
  transfers between devices with their start and end apart: 5 -> 4, of which waited for: 4 -> 2; matrix products, arithmetic and copies ran while one was open for 2% -> 5% of each run, Pallas kernels for 0% -> 18%
where the time goes in v1:
time: 121 us
  waiting for transfers between devices  39.6 us (33%)
  blocking collectives  27.5 us (23%)
  Pallas kernels  25 us (21%)
  starting transfers between devices  15.8 us (13%)
  local copies, waits for them, and re-layouts  11 us (9%)
  other arithmetic  1.54 us (1%)
    all_to_all x1, waiting for transfers between devices, local(): kv = lax.all_to_all(kv, GROUP, split_axis=0, concat_axis=0, tiled=True)  28.3 us
    all_to_all x1, blocking collectives, local(): lax.all_to_all(attended, GROUP, split_axis=0, concat_axis=0, tiled=True)  27.5 us
    pallas_call x1, Pallas kernels, span_parts(): pl.pallas_call(span_kernel, grid=(count // chunks,), in_specs=[pl.BlockSp...  14.9 us
    all_to_all x1, waiting for transfers between devices, local(): lax.all_to_all(by_owner(query_input), GROUP, split_axis=0, concat_axis=0,...  11.3 us
    reshape x6, local copies, waits for them, and re-layouts, by_owner(): x = x.reshape(rows, members, parts, width)  6.45 us
    all_to_all x1, starting transfers between devices, local(): lax.all_to_all(by_owner(query_input), GROUP, split_axis=0, concat_axis=0,...  6.29 us
    pallas_call x1, Pallas kernels, span_totals(): pl.pallas_call(totals_kernel, grid=(count // chunks,), in_specs=[pl.Block...  6.21 us
    ppermute x2, starting transfers between devices, next_span(): return lax.ppermute(block, 'span', [(i, i + 1) for i in range(spans - 1)])  5.81 us
  transfers between devices with their start and end apart: 4, of which 2 were waited for; matrix products, arithmetic and copies ran while one was open for 5% of the time, Pallas kernels for 18%

profile of v1, /device:TPU:0, one launch (start us, length us, event | category | flops | bytes accessed | tf_op | source)
XLA Modules:
  0.0 120.6 jit_solution(2408663825368104532)
XLA Ops:
  0.0 0.0 copy-start
  0.0 1.8 %reshape.21 = bf16[128,8,2,256]{3,2,1,0:T(2,128)(2,1)S(1)} reshape(bf16[128,4096]{1,0:T(8,128)(2,1)} %param.6) | data formatting | bytes 2097152 | tf_op jit(solution)/shard_map/reshape | solution.py:231
  1.8 0.0 copy-start.4
  1.9 1.3 %copy.7 = bf16[128,8,2,256]{3,0,1,2:T(8,128)(2,1)} copy(bf16[128,8,2,256]{3,2,1,0:T(2,128)(2,1)S(1)} %reshape.21) | data formatting | bytes 2097152 | tf_op jit(solution)/shard_map/reshape | solution.py:231
  3.2 6.3 %all-to-all-start = ((bf16[16,128,256]{2,1,0:T(8,128)(2,1)}), bf16[16,128,256]{2,1,0:T(8,128)(2,1)S(1)}, u32[]{:S(2)}, u32[]{:S(2)}) async-start(bf16[16,128,256]{2,1,0:T(8,128)(2,1)} %bitcast.1), calls=%async_computation | async-start | bytes 2097152 | tf_op jit(solution)/shard_map/all_to_all | solution.py:236
  9.5 0.0 copy-done.4
  9.5 0.8 reshape.23
  10.3 0.3 copy.8
  10.6 1.8 %reshape.24 = bf16[128,8,2,256]{3,2,1,0:T(2,128)(2,1)S(1)} reshape(bf16[128,4096]{1,0:T(8,128)(2,1)} %param.8) | data formatting | bytes 2097152 | tf_op jit(solution)/shard_map/reshape | solution.py:231
  12.5 0.3 copy.9
  12.8 1.5 %pad_maximum_fusion = bf16[16,2,128,256]{3,2,1,0:T(8,128)(2,1)} fusion(bf16[16,1,128,256]{3,2,1,0:T(8,128)(2,1)S(1)} %bitcast.25, bf16[16,1,128,256]{3,2,1,0:T(8,128)(2,1)S(1)} %bitcast.24), kind=kLoop, calls=%fused_computation | loop fusion | flops 1048576 | bytes 4194304 | tf_op jit(solution)/shard_map/stack | solution.py:234
  14.3 11.3 %all-to-all-done.q_ref = bf16[16,128,256]{2,1,0:T(8,128)(2,1)S(1)} async-done(((bf16[16,128,256]{2,1,0:T(8,128)(2,1)}), bf16[16,128,256]{2,1,0:T(8,128)(2,1)S(1)}, u32[]{:S(2)}, u32[]{:S(2)}) %all-to-all-start) | async-done | bytes 1048608 | tf_op jit(solution)/shard_map/all_to_all | solution.py:236
  25.6 3.7 %all-to-all-start.1 = ((bf16[16,2,128,256]{3,2,1,0:T(8,128)(2,1)}), bf16[16,2,128,256]{3,2,1,0:T(8,128)(2,1)S(1)}, u32[]{:S(2)}, u32[]{:S(2)}) async-start(bf16[16,2,128,256]{3,2,1,0:T(8,128)(2,1)} %pad_maximum_fusion), calls=%async_computation.1 | async-start | bytes 4194304 | tf_op jit(solution)/shard_map/all_to_all | solution.py:235
  29.4 0.0 copy-done.1
  29.4 0.8 copy.10
  30.2 0.0 copy-done.5
  30.2 0.1 dynamic_slice.7
  30.3 0.0 copy-done
  30.3 28.3 %all-to-all-done.1.k_ref.v_ref = bf16[16,2,128,256]{3,2,1,0:T(8,128)(2,1)S(1)} async-done(((bf16[16,2,128,256]{3,2,1,0:T(8,128)(2,1)}), bf16[16,2,128,256]{3,2,1,0:T(8,128)(2,1)S(1)}, u32[]{:S(2)}, u32[]{:S(2)}) %all-to-all-start.1) | async-done | bytes 2097184 | tf_op jit(solution)/shard_map/all_to_all | solution.py:235
  58.6 4.5 %collective-permute-start = (bf16[3,16,256]{2,1,0:T(8,128)(2,1)S(1)}, bf16[3,16,256]{2,1,0:T(8,128)(2,1)S(1)}, u32[]{:S(2)}, u32[]{:S(2)}) collective-permute-start(bf16[3,16,256]{2,1,0:T(8,128)(2,1)S(1)} %pad_maximum_fusion.1), channel_id=1, source_target_pairs={{0,16},{1,17},{2,18},{3,19},{4,20},{5,21},{6,22},{7,23},{8,24},{9,... | collective-permute-start | bytes 73736 | tf_op jit(solution)/shard_map/ppermute | solution.py:221
  63.1 0.0 copy-start.2
  63.1 0.9 copy-done.2
  64.1 6.2 %shard_map.65 = bf16[2,1024,128]{2,1,0:T(8,128)(2,1)S(1)} custom-call(bf16[16,2,128,256]{3,2,1,0:T(8,128)(2,1)S(1)} %all-to-all-done.1.k_ref.v_ref, bf16[16,2,128,256]{3,2,1,0:T(8,128)(2,1)S(1)} %all-to-all-done.1.k_ref.v_ref, bf16[2,16,256]{2,1,0:T(8,128)(2,1)S(1)} %broadcast_in_dim.6.halo_ref, f32[3,4,256]{2,1,0:T(4,128)S(1)} %constant_dynamic-slice_fusion.w_ref, ...), custom_call_target="tpu_custom_call" | custom-call | flops 4294967296 | bytes 4194304 | tf_op jit(solution)/shard_map/pallas_call | solution.py:146
  70.3 1.3 %collective-permute-start.1 = (bf16[2,1024,128]{2,1,0:T(8,128)(2,1)S(1)}, bf16[2,1024,128]{2,1,0:T(8,128)(2,1)S(1)}, u32[]{:S(2)}, u32[]{:S(2)}) collective-permute-start(bf16[2,1024,128]{2,1,0:T(8,128)(2,1)S(1)} %shard_map.65), channel_id=1, source_target_pairs={{0,16},{1,17},{2,18},{3,19},{4,20},{5,21},{6,22},{7,23},{8,24},{9,... | collective-permute-start | bytes 1572872 | tf_op jit(solution)/shard_map/ppermute | solution.py:221
  71.6 0.0 collective-permute-done
  71.7 0.0 copy-done.3
  71.7 14.9 %shard_map.64 = (f32[2048,256]{1,0:T(8,128)S(1)}, bf16[2,2048,1024]{2,1,0:T(8,128)(2,1)S(1)}) custom-call(bf16[16,128,256]{2,1,0:T(8,128)(2,1)S(1)} %all-to-all-done.q_ref, bf16[16,2,128,256]{3,2,1,0:T(8,128)(2,1)S(1)} %all-to-all-done.1.k_ref.v_ref, bf16[16,2,128,256]{3,2,1,0:T(8,128)(2,1)S(1)} %all-to-all-done.1.k_ref.v_ref, ...), custom_call_target="tpu_custom_call" | custom-call | flops 10737418240 | bytes 12582912 | tf_op jit(solution)/shard_map/pallas_call | solution.py:172
  86.6 0.0 collective-permute-done.1.state_ref
  86.6 3.8 %shard_map.66 = bf16[2048,256]{1,0:T(8,128)(2,1)S(1)} custom-call(f32[2048,256]{1,0:T(8,128)S(1)} %get-tuple-element.7.part_ref, bf16[2,2048,1024]{2,1,0:T(8,128)(2,1)S(1)} %get-tuple-element.8.feat_ref, bf16[2,1024,128]{2,1,0:T(8,128)(2,1)S(1)} %collective-permute-done.1.state_ref, f32[1,256]{1,0:T(1,128)S(1)} %bitcast.21), custom_call_target="tpu_custom_call" | custom-call | flops 1073741824 | bytes 12582912 | tf_op jit(solution)/shard_map/pallas_call | solution.py:202
  90.5 27.5 %all_to_all.15 = bf16[16,128,256]{2,1,0:T(8,128)(2,1)S(1)} all-to-all(bf16[16,128,256]{2,1,0:T(8,128)(2,1)S(1)} %bitcast.18), channel_id=1, replica_groups=mesh['span'=2,'part'=2,'sp'=8] {'part','sp'}, dimensions={0} | all-to-all | bytes 2097152 | tf_op jit(solution)/shard_map/all_to_all | solution.py:261
  117.9 1.1 copy.13
  119.0 1.6 %reshape.27 = bf16[128,4096]{1,0:T(8,128)(2,1)} reshape(bf16[128,8,2,256]{3,2,1,0:T(2,128)(2,1)S(1)} %bitcast.23) | data formatting | bytes 2097152 | tf_op jit(solution)/shard_map/reshape | solution.py:263
  (10 shorter events, 0.0 us)
Async XLA Ops:
  0.0 30.3 %copy-start = (f32[3,4,512]{2,1,0:T(4,128)S(1)}, f32[3,4,512]{2,1,0:T(4,128)}, u32[]{:S(2)}) copy-start(f32[3,4,512]{2,1,0:T(4,128)} %param.9) | copy-start | bytes 73732
  1.8 7.6 %copy-start.4 = (bf16[128,4096]{1,0:T(8,128)(2,1)S(1)}, bf16[128,4096]{1,0:T(8,128)(2,1)}, u32[]{:S(2)}) copy-start(bf16[128,4096]{1,0:T(8,128)(2,1)} %param.7) | copy-start | bytes 3145732
  3.2 22.5 %all-to-all-start = ((bf16[16,128,256]{2,1,0:T(8,128)(2,1)}), bf16[16,128,256]{2,1,0:T(8,128)(2,1)S(1)}, u32[]{:S(2)}, u32[]{:S(2)}) async-start(bf16[16,128,256]{2,1,0:T(8,128)(2,1)} %bitcast.1), calls=%async_computation | async-start | bytes 2097152 | tf_op jit(solution)/shard_map/all_to_all | solution.py:236
  14.3 15.0 %copy-start.1 = (bf16[128,1024]{1,0:T(8,128)(2,1)S(1)}, bf16[128,1024]{1,0:T(8,128)(2,1)}, u32[]{:S(2)}) copy-start(bf16[128,1024]{1,0:T(8,128)(2,1)} %map_ref.1) | copy-start | bytes 786436
  14.3 15.9 %copy-start.5 = (f32[512]{0:T(512)S(1)}, f32[512]{0:T(512)}, u32[]{:S(2)}) copy-start(f32[512]{0:T(512)} %param.11) | copy-start | bytes 6148
  25.6 33.0 %all-to-all-start.1 = ((bf16[16,2,128,256]{3,2,1,0:T(8,128)(2,1)}), bf16[16,2,128,256]{3,2,1,0:T(8,128)(2,1)S(1)}, u32[]{:S(2)}, u32[]{:S(2)}) async-start(bf16[16,2,128,256]{3,2,1,0:T(8,128)(2,1)} %pad_maximum_fusion), calls=%async_computation.1 | async-start | bytes 4194304 | tf_op jit(solution)/shard_map/all_to_all | solution.py:235
  58.6 13.0 %collective-permute-start = (bf16[3,16,256]{2,1,0:T(8,128)(2,1)S(1)}, bf16[3,16,256]{2,1,0:T(8,128)(2,1)S(1)}, u32[]{:S(2)}, u32[]{:S(2)}) collective-permute-start(bf16[3,16,256]{2,1,0:T(8,128)(2,1)S(1)} %pad_maximum_fusion.1), channel_id=1, source_target_pairs={{0,16},{1,17},{2,18},{3,19},{4,20},{5,21},{6,22},{7,23},{8,24},{9,... | collective-permute-start | bytes 73736 | tf_op jit(solution)/shard_map/ppermute | solution.py:221
  63.1 1.0 copy-start.2
  64.1 7.6 %copy-start.3 = (bf16[128,1024]{0,1:T(8,128)(2,1)S(1)}, bf16[128,1024]{0,1:T(8,128)(2,1)}, u32[]{:S(2)}) copy-start(bf16[128,1024]{0,1:T(8,128)(2,1)} %copy.10) | copy-start | bytes 786436
  70.3 16.3 %collective-permute-start.1 = (bf16[2,1024,128]{2,1,0:T(8,128)(2,1)S(1)}, bf16[2,1024,128]{2,1,0:T(8,128)(2,1)S(1)}, u32[]{:S(2)}, u32[]{:S(2)}) collective-permute-start(bf16[2,1024,128]{2,1,0:T(8,128)(2,1)S(1)} %shard_map.65), channel_id=1, source_target_pairs={{0,16},{1,17},{2,18},{3,19},{4,20},{5,21},{6,22},{7,23},{8,24},{9,... | collective-permute-start | bytes 1572872 | tf_op jit(solution)/shard_map/ppermute | solution.py:221
